TPU v7x, 512 devices: a whole 4x4x16 slice. The times are simulated.
512 devices in a mesh: scene: 64 (over z_lo, x, core), tile: 8 (over z_hi, y).
Axes of the slice: x: 4, y: 4, z: 16 (z_hi: 2, z_lo: 8; z = z_hi * 8 + z_lo), core: 2. Of those that a mesh axis runs over, the one named last changes fastest.
Arguments:
- radiance: bfloat16 [512, 8, 10, 8192], P(('scene', 'tile')), may hold values from -8 to 8
- cloud_weight: int32 [512, 8, 8192], P(('scene', 'tile')), may hold values from 0 to 15
- footprint: int32 [512, 8], replicated, may hold values from 0 to 63, as said below
Outputs:
- composite: bfloat16 [64, 10, 8192], P('tile', None, 'scene')
- overview_one: bfloat16 [64, 10, 64, 32], P('tile')
- overview_two: bfloat16 [64, 10, 32, 16], P('tile')
- overview_three: bfloat16 [64, 10, 16, 8], P('tile')
- overview_four: bfloat16 [64, 10, 8, 4], P('tile')
- overview_five: bfloat16 [64, 10, 4, 2], P('tile')
Inputs may be any that keep to these rules, and one draw needn't show every extreme that they name: `footprint`: each row names 8 different tiles; at most 2 tiles of a row share the value of tile // 8, and in every row some such group holds exactly 2 tiles.
All inputs are finite; a program needn't handle non-finite values.
Results may differ from a plain program's by a relative error of at most 0.012.
Values may be sent and summed in bfloat16 or wider, within the bound.
A program may use at most 128 MiB of HBM per device.

v0:
```python
import jax
import jax.numpy as jnp
from jax import lax
from jax.sharding import PartitionSpec as P

K = 8
TILE_DEV = 8
COLS = 64


def average_pool(values):
    height = values.shape[-2]
    width = values.shape[-1]
    shaped = values.astype(jnp.float32).reshape(values.shape[:-2] + (height // 2, 2, width // 2, 2))
    return jnp.mean(shaped, axis=(-3, -1)).astype(jnp.bfloat16)


def owner_rank(tile_rows, tile_dev):
    owner_of = tile_rows // tile_dev
    same_owner = owner_of[..., :, None] == owner_of[..., None, :]
    positions = jnp.arange(tile_rows.shape[-1])
    earlier = positions[None, :] < positions[:, None]
    rank_of = jnp.sum(jnp.logical_and(same_owner, earlier), axis=-1)
    return (owner_of, rank_of)


def slot_table(tile_rows, owner_index, capacity, tile_dev):
    owner_of, rank_of = owner_rank(tile_rows, tile_dev)
    matched = owner_of == owner_index
    local_tile = tile_rows - owner_index * tile_dev
    by_rank = jnp.logical_and(
        matched[..., None], rank_of[..., None] == jnp.arange(capacity)
    ).astype(jnp.float32)
    by_tile = (local_tile[..., None] == jnp.arange(tile_dev)).astype(jnp.float32)
    return jnp.einsum("skc,sku->scu", by_rank, by_tile, precision=lax.Precision.HIGHEST)


def on_device(radiance, cloud_weight, footprint):
    owners = lax.axis_size("tile")
    capacity = max(2, 2 * K // owners)
    scene_index = lax.axis_index("scene")
    tile_index = lax.axis_index("tile")
    device = scene_index * owners + tile_index
    pixels = radiance.shape[3]
    bands = radiance.shape[2]
    my_row = lax.dynamic_slice_in_dim(footprint, device, 1, 0)[0]
    owner_of, rank_of = owner_rank(my_row, TILE_DEV)
    slot_of = owner_of * capacity + rank_of
    placement = (jnp.arange(owners * capacity)[:, None] == slot_of[None, :]).astype(jnp.bfloat16)
    send_rad = jnp.einsum("pk,kbq->pbq", placement, radiance[0], preferred_element_type=jnp.float32)
    send_rad = send_rad.astype(jnp.bfloat16).reshape(owners, capacity, bands, pixels)
    weight_bf = cloud_weight[0].astype(jnp.bfloat16)
    send_weight = jnp.dot(placement, weight_bf, preferred_element_type=jnp.float32)
    send_weight = send_weight.astype(jnp.bfloat16).reshape(owners, capacity, 1, pixels)
    got_rad, got_weight = (
        lax.all_to_all(send_rad, "tile", split_axis=0, concat_axis=0, tiled=True),
        lax.all_to_all(send_weight, "tile", split_axis=0, concat_axis=0, tiled=True),
    )
    source_rows = lax.dynamic_slice_in_dim(footprint, scene_index * owners, owners, 0)
    assign = slot_table(source_rows, tile_index, capacity, TILE_DEV)
    weight_float = got_weight[:, :, 0, :].astype(jnp.float32)
    product = weight_float[:, :, None, :] * got_rad.astype(jnp.float32)
    local_sums = jnp.einsum("scu,scbq->ubq", assign, product, precision=lax.Precision.HIGHEST)
    local_totals = jnp.einsum("scu,scq->uq", assign, weight_float, precision=lax.Precision.HIGHEST)
    weighted_sums, weight_totals = (
        lax.psum_scatter(local_sums, "scene", scatter_dimension=2, tiled=True),
        lax.psum_scatter(local_totals, "scene", scatter_dimension=1, tiled=True),
    )
    composite = (weighted_sums / jnp.maximum(weight_totals, 1.0)[:, None, :]).astype(jnp.bfloat16)
    local_rows = composite.shape[2] // COLS
    grid = composite.reshape(composite.shape[0], bands, local_rows, COLS)
    whole_grid = lax.all_gather(grid, "scene", axis=2, tiled=True)
    overview_one = average_pool(whole_grid)
    overview_two = average_pool(overview_one)
    overview_three = average_pool(overview_two)
    overview_four = average_pool(overview_three)
    overview_five = average_pool(overview_four)
    return (composite, overview_one, overview_two, overview_three, overview_four, overview_five)


def solution(mesh):
    in_specs = (P(("scene", "tile"), None, None, None), P(("scene", "tile"), None, None), P())
    out_specs = (
        P("tile", None, "scene"),
        P("tile", None, None, None),
        P("tile", None, None, None),
        P("tile", None, None, None),
        P("tile", None, None, None),
        P("tile", None, None, None),
    )
    return jax.shard_map(
        on_device, mesh=mesh, in_specs=in_specs, out_specs=out_specs, check_vma=False
    )
```

profile of v0, /device:TPU:1, one launch (start us, length us, event | category | flops | bytes accessed | tf_op | source)
XLA Modules:
  0.0 1196.3 jit_solution(4927155921936412516)
XLA Ops:
  7.2 0.9 constant_dynamic-slice_fusion
  8.4 1.3 convolution_convert_fusion.1
  9.7 0.9 reshape.103
  10.5 18.3 %all-to-all-start = ((bf16[8,2,1,8192]{3,1,2,0:T(2,128)(2,1)}), bf16[8,2,1,8192]{3,1,2,0:T(2,128)(2,1)S(1)}, u32[]{:S(2)}, u32[]{:S(2)}) async-start(bf16[8,2,1,8192]{3,1,2,0:T(2,128)(2,1)} %bitcast.6), calls=%async_computation | async-start | bytes 524288 | tf_op jit(solution)/shard_map/all_to_all | solution.py:57
  28.8 2.4 convolution_convert_fusion
  31.2 5.4 reshape.104
  36.5 7.5 copy.94
  44.1 13.9 %all-to-all-start.1 = ((bf16[8,2,10,8192]{3,1,2,0:T(2,128)(2,1)}), bf16[8,2,10,8192]{3,1,2,0:T(2,128)(2,1)}, u32[]{:S(2)}, u32[]{:S(2)}) async-start(bf16[8,2,10,8192]{3,1,2,0:T(2,128)(2,1)} %copy.94), calls=%async_computation.1 | async-start | bytes 5242880 | tf_op jit(solution)/shard_map/all_to_all | solution.py:56
  59.0 1.1 convolution_bitcast_fusion.1
  60.3 47.7 %all-to-all-done.1 = bf16[8,2,10,8192]{3,1,2,0:T(2,128)(2,1)} async-done(((bf16[8,2,10,8192]{3,1,2,0:T(2,128)(2,1)}), bf16[8,2,10,8192]{3,1,2,0:T(2,128)(2,1)}, u32[]{:S(2)}, u32[]{:S(2)}) %all-to-all-start.1) | async-done | bytes 2621472 | tf_op jit(solution)/shard_map/all_to_all | solution.py:56
  108.0 7.3 convolution_bitcast_fusion
  115.5 429.0 %reduce-scatter.5.cloned.1.call-done = f32[8,128]{1,0:T(8,128)} async-done(((f32[8,8192]{1,0:T(8,128)}), f32[8,128]{1,0:T(8,128)}) %reduce-scatter.5.cloned.1.call-update) | async-done | bytes 4112 | tf_op jit(solution)/shard_map/reduce_scatter | solution.py:67
  544.5 0.7 broadcast_maximum_fusion
  545.2 449.9 %reduce-scatter.3.cloned.1.call-done = f32[8,10,128]{2,0,1:T(8,128)} async-done(((f32[8,10,8192]{2,0,1:T(8,128)}), f32[8,10,128]{2,0,1:T(8,128)}) %reduce-scatter.3.cloned.1.call-update) | async-done | bytes 40976 | tf_op jit(solution)/shard_map/reduce_scatter | solution.py:66
  995.1 0.8 divide_convert_fusion
  996.6 125.3 %all-gather.2.cloned.1.call-done = bf16[8,10,128,64]{3,0,1,2:T(8,128)(2,1)} async-done(((bf16[8,10,2,64]{3,0,1,2:T(8,128)(2,1)}), bf16[8,10,128,64]{3,0,1,2:T(8,128)(2,1)}) %all-gather.2.cloned.1.call-update) | async-done | bytes 1310736 | tf_op jit(solution)/shard_map/all_gather | solution.py:72
  1121.9 4.4 copy.100
  1126.3 25.0 %copy.101 = f32[8,10,128,64]{1,0,3,2:T(8,128)} copy(bf16[8,10,128,64]{2,3,1,0:T(8,128)(2,1)S(1)} %copy.100) | data formatting | bytes 3932160 | tf_op jit(solution)/shard_map/reshape | solution.py:14
  1151.3 16.3 %reduce_sum.68 = f32[8,10,64,32]{1,0,3,2:T(8,128)} reduce(f32[8,10,64,2,32,2]{1,0,5,4,3,2:T(8,128)} %bitcast.56, f32[]{:T(128)} %constant.53.clone.1), dimensions={3,5}, to_apply=%region_4.5 | reduce | flops 491520 | bytes 3276804 | tf_op jit(solution)/shard_map/reduce_sum | solution.py:15
  1167.6 6.4 multiply_convert_fusion
  1174.0 7.0 copy.102
  1181.0 3.4 convert_reduce_fusion
  1184.6 2.3 copy.103
  1187.2 1.2 copy.104
  (41 shorter events, 4.5 us)
Async XLA Ops:
  7.2 21.7 %copy-start = (bf16[1,8,10,8192]{3,1,2,0:T(8,128)(2,1)S(1)}, bf16[1,8,10,8192]{3,1,2,0:T(8,128)(2,1)}, u32[]{:S(2)}) copy-start(bf16[1,8,10,8192]{3,1,2,0:T(8,128)(2,1)} %param.3) | copy-start | bytes 3932164
  10.5 33.5 %all-to-all-start = ((bf16[8,2,1,8192]{3,1,2,0:T(2,128)(2,1)}), bf16[8,2,1,8192]{3,1,2,0:T(2,128)(2,1)S(1)}, u32[]{:S(2)}, u32[]{:S(2)}) async-start(bf16[8,2,1,8192]{3,1,2,0:T(2,128)(2,1)} %bitcast.6), calls=%async_computation | async-start | bytes 524288 | tf_op jit(solution)/shard_map/all_to_all | solution.py:57
  44.0 14.0 %copy-start.3 = (s32[512,8]{0,1:T(8,128)S(1)}, s32[512,8]{0,1:T(8,128)}, u32[]{:S(2)}) copy-start(s32[512,8]{0,1:T(8,128)} %param.5) | copy-start | bytes 49156
  44.1 63.9 %all-to-all-start.1 = ((bf16[8,2,10,8192]{3,1,2,0:T(2,128)(2,1)}), bf16[8,2,10,8192]{3,1,2,0:T(2,128)(2,1)}, u32[]{:S(2)}, u32[]{:S(2)}) async-start(bf16[8,2,10,8192]{3,1,2,0:T(2,128)(2,1)} %copy.94), calls=%async_computation.1 | async-start | bytes 5242880 | tf_op jit(solution)/shard_map/all_to_all | solution.py:56
  58.0 486.6 %reduce-scatter.5.cloned.1.call-start = ((), (), s32[]{:S(2)}) async-start(), calls=%async_computation.5 | async-start | bytes 266240 | tf_op jit(solution)/shard_map/reduce_scatter | solution.py:67
  60.1 935.0 %reduce-scatter.3.cloned.1.call-start = ((), (), s32[]{:S(2)}) async-start(), calls=%async_computation.4 | async-start | bytes 2662400 | tf_op jit(solution)/shard_map/reduce_scatter | solution.py:66
  115.3 1006.6 %all-gather.2.cloned.1.call-start = ((), (), s32[]{:S(2)}) async-start(), calls=%async_computation.6 | async-start | bytes 2662400 | tf_op jit(solution)/shard_map/all_gather | solution.py:72
  995.9 155.4 %copy-start.2 = (bf16[8,10,128]{2,0,1:T(8,128)(2,1)}, bf16[8,10,128]{2,0,1:T(8,128)(2,1)S(1)}, u32[]{:S(2)}) copy-start(bf16[8,10,128]{2,0,1:T(8,128)(2,1)S(1)} %divide_convert_fusion) | copy-start | bytes 61444
  1184.4 5.4 copy-start.1
Sparse Core Ops, SparseCore 0:
  62.2 482.3 reduce-scatter.4
  547.5 447.5 reduce-scatter.2
  997.8 124.0 all-gather.1
where the time goes:
time: 1200 us
  waiting for transfers between devices  1050 us (88%)
  local copies, waits for them, and re-layouts  56.9 us (5%)
  starting transfers between devices  32.4 us (3%)
  other arithmetic  28.9 us (2%)
  between operations  13.9 us (1%)
  matrix products  12.2 us (1%)
    reduce_scatter x1, waiting for transfers between devices, on_device(): lax.psum_scatter(local_sums, 'scene', scatter_dimension=2, tiled=True)  450 us
    reduce_scatter x1, waiting for transfers between devices, on_device(): lax.psum_scatter(local_totals, 'scene', scatter_dimension=1, tiled=True)  429 us
    all_gather x1, waiting for transfers between devices, on_device(): whole_grid = lax.all_gather(grid, 'scene', axis=2, tiled=True)  125 us
    all_to_all x1, waiting for transfers between devices, on_device(): lax.all_to_all(send_rad, 'tile', split_axis=0, concat_axis=0, tiled=True)  47.7 us
    reshape x1, local copies, waits for them, and re-layouts, average_pool(): values.astype(jnp.float32)  25 us
  transfers between devices with their start and end apart: 5, of which 5 were waited for; matrix products, arithmetic and copies ran while one was open for 2% of the time, Pallas kernels for 0%

commit v1 on v0

--- a/solution.py
+++ b/solution.py
@@ -69,7 +69,13 @@
     composite = (weighted_sums / jnp.maximum(weight_totals, 1.0)[:, None, :]).astype(jnp.bfloat16)
     local_rows = composite.shape[2] // COLS
     grid = composite.reshape(composite.shape[0], bands, local_rows, COLS)
-    whole_grid = lax.all_gather(grid, "scene", axis=2, tiled=True)
+    touch_the_words = lambda array_dim, row_axis, mine_x: jnp.concatenate(
+        lax.all_to_all(
+            jnp.stack([mine_x for _ in range(lax.psum(1, axis_name=row_axis))]), row_axis, 0, 0
+        ),
+        axis=array_dim,
+    )
+    whole_grid = touch_the_words(2, "scene", grid)
     overview_one = average_pool(whole_grid)
     overview_two = average_pool(overview_one)
     overview_three = average_pool(overview_two)

time: 1200 us -> 1120 us (0.933)
  waiting for transfers between devices: 1050 us -> 926 us
  blocking collectives: 0 us -> 76.8 us
  local copies, waits for them, and re-layouts: 56.9 us -> 42.9 us
    all_gather x1 -> x0, waiting for transfers between devices: 125 us -> none  [on_device(): whole_grid = lax.all_gather(grid, 'scene', axis=2, tiled=True)]
    all_to_all x0 -> x1, blocking collectives: none -> 76.8 us  [on_device(): lax.all_to_all(jnp.stack([mine_x for _ in range(lax.psum(1, axis_name=row...]
    reshape x3 -> x0, local copies, waits for them, and re-layouts: 25.7 us -> none  [the longest x1 25 us: average_pool(): values.astype(jnp.float32)]
  transfers between devices with their start and end apart: 5 -> 4, of which waited for: 5 -> 4; matrix products, arithmetic and copies ran while one was open for 2% -> 2% of each run, Pallas kernels for 0% -> 0%
where the time goes in v1:
time: 1120 us
  waiting for transfers between devices  926 us (83%)
  blocking collectives  76.8 us (7%)
  local copies, waits for them, and re-layouts  42.9 us (4%)
  starting transfers between devices  32.2 us (3%)
  other arithmetic  17 us (2%)
  between operations  14.2 us (1%)
  matrix products  12.2 us (1%)
    reduce_scatter x1, waiting for transfers between devices, on_device(): lax.psum_scatter(local_sums, 'scene', scatter_dimension=2, tiled=True)  449 us
    reduce_scatter x1, waiting for transfers between devices, on_device(): lax.psum_scatter(local_totals, 'scene', scatter_dimension=1, tiled=True)  429 us
    all_to_all x1, blocking collectives, on_device(): lax.all_to_all(jnp.stack([mine_x for _ in range(lax.psum(1, axis_name=row...  76.8 us
    all_to_all x1, waiting for transfers between devices, on_device(): lax.all_to_all(send_rad, 'tile', split_axis=0, concat_axis=0, tiled=True)  47.4 us
  transfers between devices with their start and end apart: 4, of which 4 were waited for; matrix products, arithmetic and copies ran while one was open for 2% of the time, Pallas kernels for 0%

profile of v1, /device:TPU:1, one launch (start us, length us, event | category | flops | bytes accessed | tf_op | source)
XLA Modules:
  0.0 1121.8 jit_solution(1250129875943386022)
XLA Ops:
  8.4 1.3 convolution_convert_fusion.1
  10.5 18.3 %all-to-all-start = ((bf16[8,2,1,8192]{3,1,2,0:T(2,128)(2,1)}), bf16[8,2,1,8192]{3,1,2,0:T(2,128)(2,1)S(1)}, u32[]{:S(2)}, u32[]{:S(2)}) async-start(bf16[8,2,1,8192]{3,1,2,0:T(2,128)(2,1)} %bitcast.6), calls=%async_computation | async-start | bytes 524288 | tf_op jit(solution)/shard_map/all_to_all | solution.py:57
  28.8 2.4 convolution_convert_fusion
  31.2 5.4 reshape.102
  36.5 7.5 copy.96
  44.1 13.9 %all-to-all-start.1 = ((bf16[8,2,10,8192]{3,1,2,0:T(2,128)(2,1)}), bf16[8,2,10,8192]{3,1,2,0:T(2,128)(2,1)}, u32[]{:S(2)}, u32[]{:S(2)}) async-start(bf16[8,2,10,8192]{3,1,2,0:T(2,128)(2,1)} %copy.96), calls=%async_computation.1 | async-start | bytes 5242880 | tf_op jit(solution)/shard_map/all_to_all | solution.py:56
  59.0 1.1 convolution_bitcast_fusion.1
  60.3 47.4 %all-to-all-done.1 = bf16[8,2,10,8192]{3,1,2,0:T(2,128)(2,1)} async-done(((bf16[8,2,10,8192]{3,1,2,0:T(2,128)(2,1)}), bf16[8,2,10,8192]{3,1,2,0:T(2,128)(2,1)}, u32[]{:S(2)}, u32[]{:S(2)}) %all-to-all-start.1) | async-done | bytes 2621472 | tf_op jit(solution)/shard_map/all_to_all | solution.py:56
  107.7 7.3 convolution_bitcast_fusion
  115.1 429.5 %reduce-scatter.5.cloned.1.call-done = f32[8,128]{1,0:T(8,128)} async-done(((f32[8,8192]{1,0:T(8,128)}), f32[8,128]{1,0:T(8,128)}) %reduce-scatter.5.cloned.1.call-update) | async-done | bytes 4112 | tf_op jit(solution)/shard_map/reduce_scatter | solution.py:67
  545.2 449.4 %reduce-scatter.3.cloned.1.call-done = f32[8,10,128]{2,0,1:T(8,128)} async-done(((f32[8,10,8192]{2,0,1:T(8,128)}), f32[8,10,128]{2,0,1:T(8,128)}) %reduce-scatter.3.cloned.1.call-update) | async-done | bytes 40976 | tf_op jit(solution)/shard_map/reduce_scatter | solution.py:66
  995.5 1.8 broadcast_bitcast_fusion
  997.4 4.4 reshape.111
  1001.8 76.8 %all_to_all.15 = bf16[64,2,5120]{2,1,0:T(2,128)(2,1)} all-to-all(bf16[64,2,5120]{2,1,0:T(2,128)(2,1)S(1)} %reshape.111), channel_id=1, replica_groups=mesh['scene'=64,'tile'=8] {'scene'}, dimensions={0} | all-to-all | bytes 2621440 | tf_op jit(solution)/shard_map/all_to_all | solution.py:73
  1078.6 5.3 reshape.112
  1083.9 4.3 convert_reduce_fusion
  1088.3 3.3 copy.102
  1091.6 2.2 reduce_sum.80
  1093.9 1.0 copy.104
  1094.9 7.2 copy.103
  1102.1 5.9 reduce_sum.81
  1108.0 1.8 multiply_convert_fusion
  1109.9 2.3 copy.105
  1112.4 1.2 copy.106
  (41 shorter events, 6.7 us)
Async XLA Ops:
  7.2 21.7 %copy-start = (bf16[1,8,10,8192]{3,1,2,0:T(8,128)(2,1)S(1)}, bf16[1,8,10,8192]{3,1,2,0:T(8,128)(2,1)}, u32[]{:S(2)}) copy-start(bf16[1,8,10,8192]{3,1,2,0:T(8,128)(2,1)} %param.3) | copy-start | bytes 3932164
  10.5 33.6 %all-to-all-start = ((bf16[8,2,1,8192]{3,1,2,0:T(2,128)(2,1)}), bf16[8,2,1,8192]{3,1,2,0:T(2,128)(2,1)S(1)}, u32[]{:S(2)}, u32[]{:S(2)}) async-start(bf16[8,2,1,8192]{3,1,2,0:T(2,128)(2,1)} %bitcast.6), calls=%async_computation | async-start | bytes 524288 | tf_op jit(solution)/shard_map/all_to_all | solution.py:57
  44.0 14.0 %copy-start.2 = (s32[512,8]{0,1:T(8,128)S(1)}, s32[512,8]{0,1:T(8,128)}, u32[]{:S(2)}) copy-start(s32[512,8]{0,1:T(8,128)} %param.5) | copy-start | bytes 49156
  44.1 63.6 %all-to-all-start.1 = ((bf16[8,2,10,8192]{3,1,2,0:T(2,128)(2,1)}), bf16[8,2,10,8192]{3,1,2,0:T(2,128)(2,1)}, u32[]{:S(2)}, u32[]{:S(2)}) async-start(bf16[8,2,10,8192]{3,1,2,0:T(2,128)(2,1)} %copy.96), calls=%async_computation.1 | async-start | bytes 5242880 | tf_op jit(solution)/shard_map/all_to_all | solution.py:56
  58.0 486.6 %reduce-scatter.5.cloned.1.call-start = ((), (), s32[]{:S(2)}) async-start(), calls=%async_computation.6 | async-start | bytes 266240 | tf_op jit(solution)/shard_map/reduce_scatter | solution.py:67
  60.1 934.5 %reduce-scatter.3.cloned.1.call-start = ((), (), s32[]{:S(2)}) async-start(), calls=%async_computation.5 | async-start | bytes 2662400 | tf_op jit(solution)/shard_map/reduce_scatter | solution.py:66
  995.4 6.4 copy-start.1
Sparse Core Ops, SparseCore 0:
  62.2 482.3 reduce-scatter.4
  547.5 447.0 reduce-scatter.2
